TPU v7x, 512 devices: a whole 4x8x8 slice. The times are simulated.
512 devices in a mesh: cam: 8 (over y_hi, core), frame: 64 (over x, y_lo, z).
Axes of the slice: x: 4, y: 8 (y_hi: 4, y_lo: 2; y = y_hi * 2 + y_lo), z: 8, core: 2. Of those that a mesh axis runs over, the one named last changes fastest.
Arguments:
- qkv: bfloat16 [3, 8, 64, 128, 1152], P(None, 'cam', 'frame'), may hold values from -20 to 20
- cross_q: bfloat16 [8, 64, 128, 1152], P('cam', 'frame'), may hold values from -20 to 20
- box_kv: bfloat16 [2, 64, 64, 1152], P(None, 'frame', 'cam'), may hold values from -20 to 20
- null_kv: bfloat16 [2, 1152], replicated, may hold values from -20 to 20
- view_link: int32 [8, 2], P('cam'), may hold values 0 or 1
- box_counts: int32 [64], P('frame'), may hold values from 1 to 64, 2048 in all
- box_visible: int32 [8, 64, 64], P('cam', 'frame'), may hold values 0 or 1
Outputs:
- blended: bfloat16 [8, 64, 128, 1152], P('cam', 'frame')
Inputs may be any that keep to these rules, and one draw needn't show every extreme that they name: `box_counts`: some frame has all 64 slots filled.
All inputs are finite; a program needn't handle non-finite values. No bound on the sum of `view_link` or of `box_counts` or of `box_visible` on one device may be relied on, other than what follows from the above.
Results may differ from a plain program's by a relative error of at most 0.0045.
Values may be sent and summed in bfloat16 or wider, within the bound.
A program may use at most 64 MiB of HBM per device.

v0:
```python
import math

import jax
import jax.numpy as jnp
from jax import lax
from jax.sharding import PartitionSpec as P

HEADS = 16


def from_behind(block, axis, distance):
    devices = range(lax.axis_size(axis))
    route = [((i - distance) % len(devices), i) for i in devices]
    return lax.ppermute(block, axis, route)


def attend(query_rows, key_rows, value_rows, usable, head_count):
    row_count = query_rows.shape[0]
    feature_width = query_rows.shape[1]
    head_dim = feature_width // head_count
    query_heads = query_rows.reshape(row_count, head_count, head_dim)
    key_heads = key_rows.reshape(key_rows.shape[0], head_count, head_dim)
    value_heads = value_rows.reshape(value_rows.shape[0], head_count, head_dim)
    scores = jnp.einsum(
        "rhd,khd->hrk", query_heads, key_heads, preferred_element_type=jnp.float32
    ) * (1.0 / math.sqrt(head_dim))
    scores = jnp.where(usable[None, None, :], scores, -jnp.inf)
    row_max = jnp.max(scores, axis=2, keepdims=True)
    weights = jnp.exp(scores - row_max)
    weight_sum = jnp.sum(weights, axis=2)
    packed = weights.astype(jnp.bfloat16)
    combined = jnp.einsum("hrk,khd->rhd", packed, value_heads, preferred_element_type=jnp.float32)
    return (combined / weight_sum.T[:, :, None]).reshape(row_count, feature_width)


def attend_groups(query_rows, key_rows, value_rows, usable):
    groups = 4
    heads_each = HEADS // groups
    column_count = query_rows.shape[1] // groups
    pieces = []
    for group_id in range(groups):
        start = group_id * column_count
        stop = start + column_count
        pieces.append(
            attend(
                query_rows[:, start:stop],
                key_rows[:, start:stop],
                value_rows[:, start:stop],
                usable,
                heads_each,
            )
        )
    return jnp.concatenate(pieces, 1)


def frame_attention(stacked):
    frame_count, item_count, feature_width = (stacked.shape[1], stacked.shape[2], stacked.shape[3])
    clip_frames = min(32, frame_count)
    clip_total = frame_count // clip_frames
    head_dim = feature_width // HEADS
    shaped = stacked.reshape(3, clip_total, clip_frames, item_count, HEADS, head_dim)
    scores = jnp.einsum(
        "cfihd,cgihd->cihfg", shaped[0], shaped[1], preferred_element_type=jnp.float32
    ) * (1.0 / math.sqrt(head_dim))
    row_max = jnp.max(scores, axis=4, keepdims=True)
    weights = jnp.exp(scores - row_max)
    weight_sum = jnp.sum(weights, axis=4)
    packed = weights.astype(jnp.bfloat16)
    combined = jnp.einsum(
        "cihfg,cgihd->cfihd", packed, shaped[2], preferred_element_type=jnp.float32
    )
    result = combined / jnp.transpose(weight_sum, (0, 3, 1, 2))[..., None]
    return result.reshape(frame_count, item_count, feature_width).astype(jnp.bfloat16)


def regrouped_block(received):
    merged = received[:, :, 0]
    return frame_attention(merged)[:, None]


def view_attention(own_view, view_link):
    key_value = own_view[1:3]
    left_pair = from_behind(key_value, "cam", 1)
    right_pair = from_behind(key_value, "cam", -1)
    row_count = own_view.shape[1]
    key_rows = jnp.concatenate([key_value[0], left_pair[0], right_pair[0]], 0)
    value_rows = jnp.concatenate([key_value[1], left_pair[1], right_pair[1]], 0)
    usable = jnp.concatenate(
        [
            jnp.ones((row_count,), jnp.bool_),
            jnp.broadcast_to(view_link[0, 0] == 1, (row_count,)),
            jnp.broadcast_to(view_link[0, 1] == 1, (row_count,)),
        ]
    )
    return attend_groups(own_view[0], key_rows, value_rows, usable)


def time_attention(own_view):
    frame_devices = lax.axis_size("frame")
    row_count = own_view.shape[1]
    feature_width = own_view.shape[2]
    blocked = own_view.reshape(3, 1, frame_devices, row_count // frame_devices, feature_width)
    regrouped = regrouped_block(
        lax.all_to_all(blocked, "frame", split_axis=2, concat_axis=1, tiled=True)
    )
    returned = lax.all_to_all(regrouped, "frame", split_axis=0, concat_axis=1, tiled=True)
    return returned.reshape(row_count, feature_width).astype(jnp.float32)


def on_device(qkv, cross_q, box_kv, null_kv, view_link, box_counts, box_visible):
    own_view = qkv[:, 0, 0]
    spatial = view_attention(own_view, view_link)
    temporal = time_attention(own_view)
    boxes = lax.all_gather(box_kv, "cam", axis=2, tiled=True)
    key_rows = jnp.concatenate([null_kv[0:1], boxes[0, 0]], 0)
    value_rows = jnp.concatenate([null_kv[1:2], boxes[1, 0]], 0)
    slot_ids = jnp.arange(boxes.shape[2], dtype=jnp.int32)
    live_slots = (slot_ids < box_counts[0]) & (box_visible[0, 0] == 1)
    usable = jnp.concatenate([jnp.ones((1,), jnp.bool_), live_slots])
    cross_part = attend(cross_q[0, 0], key_rows, value_rows, usable, HEADS)
    blended = (spatial + temporal + cross_part).astype(jnp.bfloat16)
    return blended[None, None]


def solution(mesh):
    return jax.shard_map(
        on_device,
        mesh=mesh,
        in_specs=(
            P(None, "cam", "frame", None, None),
            P("cam", "frame", None, None),
            P(None, "frame", "cam", None),
            P(),
            P("cam", None),
            P("frame"),
            P("cam", "frame", None),
        ),
        out_specs=P("cam", "frame", None, None),
        check_vma=False,
    )
```

profile of v0, /device:TPU:1, one launch (start us, length us, event | category | flops | bytes accessed | tf_op | source)
XLA Modules:
  0.0 112.6 jit_solution(17309471086552599468)
XLA Ops:
  0.0 1.2 %slice_bitcast_fusion = bf16[2,128,1152]{2,1,0:T(8,128)(2,1)S(1)} fusion(bf16[3,1,1,128,1152]{4,3,0,2,1:T(8,128)(2,1)} %bitcast.109), kind=kLoop, calls=%fused_computation.46 | loop fusion | bytes 1179648 | tf_op jit(solution)/shard_map/slice | solution.py:82
  1.2 5.6 %collective-permute-start = (bf16[2,128,1152]{2,1,0:T(8,128)(2,1)S(1)}, bf16[2,128,1152]{2,1,0:T(8,128)(2,1)}, u32[]{:S(2)}, u32[]{:S(2)}) collective-permute-start(bf16[2,128,1152]{2,1,0:T(8,128)(2,1)S(1)} %slice_bitcast_fusion), channel_id=1, source_target_pairs={{448,0},{0,64},{64,128},{128,192},{192,256},{256,320},{320,384},{3... | collective-permute-start | bytes 1769480 | tf_op jit(solution)/shard_map/ppermute | solution.py:14
  6.8 5.1 %collective-permute-start.1 = (bf16[2,128,1152]{2,1,0:T(8,128)(2,1)S(1)}, bf16[2,128,1152]{2,1,0:T(8,128)(2,1)}, u32[]{:S(2)}, u32[]{:S(2)}) collective-permute-start(bf16[2,128,1152]{2,1,0:T(8,128)(2,1)S(1)} %slice_bitcast_fusion), channel_id=1, source_target_pairs={{64,0},{128,64},{192,128},{256,192},{320,256},{384,320},{448,384},... | collective-permute-start | bytes 1769480 | tf_op jit(solution)/shard_map/ppermute | solution.py:14
  12.3 1.5 %copy.235 = bf16[3,1,64,2,1152]{4,3,1,0,2:T(2,128)(2,1)} copy(bf16[3,1,64,2,1152]{4,3,2,0,1:T(2,128)(2,1)S(1)} %reshape_squeeze.7) | data formatting | bytes 1769472 | tf_op jit(solution)/shard_map/reshape;squeeze | solution.py:102
  13.8 11.3 %all-to-all-start = ((bf16[3,1,64,2,1152]{4,3,1,0,2:T(2,128)(2,1)}), bf16[3,1,64,2,1152]{4,3,1,0,2:T(2,128)(2,1)S(1)}, u32[]{:S(2)}, u32[]{:S(2)}) async-start(bf16[3,1,64,2,1152]{4,3,1,0,2:T(2,128)(2,1)} %copy.235), calls=%async_computation | async-start | bytes 1769472 | tf_op jit(solution)/shard_map/all_to_all | solution.py:104
  26.2 21.8 %all_gather.3 = bf16[2,1,64,1152]{3,2,1,0:T(8,128)(2,1)S(1)} all-gather(bf16[2,1,8,1152]{3,2,1,0:T(8,128)(2,1)S(1)} %copy-done.10), channel_id=1, replica_groups=mesh['cam'=8,'frame'=64] {'cam'}, dimensions={2}, use_global_device_ids=true | all-gather | bytes 331776 | tf_op jit(solution)/shard_map/all_gather | solution.py:114
  51.1 1.4 %fusion.58 = (f32[16,128]{1,0:T(8,128)S(1)}, f32[16,128,65]{1,2,0:T(8,128)S(1)}) fusion(bf16[128,16,72]{0,2,1:T(8,128)(2,1)} %bitcast.115, bf16[64,16,72]{2,0,1:T(8,128)(2,1)} %copy.249, bf16[1,16,72]{2,0,1:T(2,128)(2,1)S(1)} %concatenate.62, pred[65]{0:T(512)(128)(4,1)S(1)} %pad_add_fusion.1), kind=kOutput, calls=%fused_computation.86 | convolution fusion | flops 19866112 | bytes 985409 | tf_op jit(solution)/shard_map/rhd,khd->hrk/dot_general | solution.py:24
  56.8 1.3 %concatenate.61 = bf16[1,16,72]{0,2,1:T(8,128)(2,1)} reshape(bf16[1152]{0:T(1024)(128)(2,1)S(1)} %get-tuple-element.5) | data formatting | bytes 4608 | tf_op jit(solution)/shard_map/concatenate | solution.py:116
  58.2 1.4 %fusion.10 = f32[128,16,72]{0,2,1:T(8,128)S(1)} fusion(f32[16,128,65]{1,2,0:T(8,128)S(1)} %get-tuple-element.34, bf16[64,16,72]{0,2,1:T(8,128)(2,1)S(1)} %bitcast.116, bf16[1,16,72]{0,2,1:T(8,128)(2,1)} %concatenate.61, f32[128,16]{0,1:T(8,128)S(1)} %bitcast.130, f32[16,128]{1,0:T(8,128)S(1)} %get-tuple-element.33), kind=kOutput, calls=%fused_computation.17 | convolution fusion | flops 19882496 | bytes 1288448 | tf_op jit(solution)/shard_map/hrk,khd->rhd/dot_general | solution.py:32
  59.9 1.1 slice_bitcast_fusion.2
  61.0 1.1 slice_bitcast_fusion.1
  62.3 1.1 fusion.53
  64.2 1.2 %fusion.54 = (bf16[384,288]{1,0:T(8,128)(2,1)}, bf16[384,288]{1,0:T(8,128)(2,1)}, bf16[384,288]{1,0:T(8,128)(2,1)S(1)}, bf16[384,288]{1,0:T(8,128)(2,1)S(1)}) fusion(bf16[384,1152]{1,0:T(8,128)(2,1)S(1)} %get-tuple-element.45), kind=kLoop, calls=%fused_computation.82 | loop fusion | bytes 1769472 | tf_op jit(solution)/shard_map/slice | solution.py:48
  65.7 1.8 %copy.227 = bf16[384,288]{0,1:T(8,128)(2,1)} copy(bf16[384,288]{1,0:T(8,128)(2,1)} %get-tuple-element.14) | data formatting | bytes 442368 | tf_op jit(solution)/shard_map/slice | solution.py:48
  67.7 1.9 %fusion.13 = f32[128,4,72]{0,2,1:T(8,128)} fusion(bf16[384,4,72]{0,2,1:T(8,128)(2,1)} %bitcast.124, f32[4,128,384]{1,2,0:T(8,128)S(1)} %get-tuple-element.42, f32[4,128]{1,0:T(4,128)S(1)} %get-tuple-element.41, f32[128,4]{0,1:T(4,128)S(1)} %bitcast.131), kind=kOutput, calls=%fused_computation.22 | convolution fusion | flops 28741632 | bytes 1159168 | tf_op jit(solution)/shard_map/hrk,khd->rhd/dot_general | solution.py:32
  69.6 1.0 copy.234
  70.6 1.1 %copy.224 = bf16[384,288]{0,1:T(8,128)(2,1)S(1)} copy(bf16[384,288]{1,0:T(8,128)(2,1)} %get-tuple-element.11) | data formatting | bytes 442368 | tf_op jit(solution)/shard_map/slice | solution.py:47
  71.7 1.8 %copy.223 = bf16[384,288]{0,1:T(8,128)(2,1)} copy(bf16[384,288]{1,0:T(8,128)(2,1)} %get-tuple-element.15) | data formatting | bytes 442368 | tf_op jit(solution)/shard_map/slice | solution.py:48
  77.9 1.1 reshape.205
  79.0 1.1 reshape.206
  80.1 1.9 %reshape.207 = bf16[2,32,2,16,72]{4,3,2,1,0:T(8,128)(2,1)} reshape(bf16[1,1,64,2,1152]{4,3,1,0,2:T(2,128)(2,1)S(1)} %get-tuple-element.7) | data formatting | bytes 589824 | tf_op jit(solution)/shard_map/squeeze | solution.py:70
  84.6 1.6 %reshape.208 = bf16[64,1,2,1152]{3,2,1,0:T(2,128)(2,1)} reshape(bf16[2,32,2,16,72]{4,3,2,1,0:T(8,128)(2,1)S(1)} %copy.263) | data formatting | bytes 589824 | tf_op jit(solution)/shard_map/convert_element_type | solution.py:73
  86.2 13.1 %all-to-all-start.1 = ((bf16[64,1,2,1152]{3,2,1,0:T(2,128)(2,1)}), bf16[64,1,2,1152]{3,2,1,0:T(2,128)(2,1)S(1)}, u32[]{:S(2)}, u32[]{:S(2)}) async-start(bf16[64,1,2,1152]{3,2,1,0:T(2,128)(2,1)} %reshape.208), calls=%async_computation.1 | async-start | bytes 589824 | tf_op jit(solution)/shard_map/all_to_all | solution.py:106
  101.0 10.8 %all-to-all-done.1 = bf16[64,1,2,1152]{3,2,1,0:T(2,128)(2,1)S(1)} async-done(((bf16[64,1,2,1152]{3,2,1,0:T(2,128)(2,1)}), bf16[64,1,2,1152]{3,2,1,0:T(2,128)(2,1)S(1)}, u32[]{:S(2)}, u32[]{:S(2)}) %all-to-all-start.1) | async-done | bytes 294944 | tf_op jit(solution)/shard_map/all_to_all | solution.py:106
  (82 shorter events, 18.0 us)
Async XLA Ops:
  0.0 11.9 %copy-start = (bf16[3,1,1,128,1152]{4,3,2,1,0:T(8,128)(2,1)S(1)}, bf16[3,1,1,128,1152]{4,3,2,1,0:T(8,128)(2,1)}, u32[]{:S(2)}) copy-start(bf16[3,1,1,128,1152]{4,3,2,1,0:T(8,128)(2,1)} %param.7) | copy-start | bytes 2654212
  1.2 58.7 %collective-permute-start = (bf16[2,128,1152]{2,1,0:T(8,128)(2,1)S(1)}, bf16[2,128,1152]{2,1,0:T(8,128)(2,1)}, u32[]{:S(2)}, u32[]{:S(2)}) collective-permute-start(bf16[2,128,1152]{2,1,0:T(8,128)(2,1)S(1)} %slice_bitcast_fusion), channel_id=1, source_target_pairs={{448,0},{0,64},{64,128},{128,192},{192,256},{256,320},{320,384},{3... | collective-permute-start | bytes 1769480 | tf_op jit(solution)/shard_map/ppermute | solution.py:14
  6.8 54.2 %collective-permute-start.1 = (bf16[2,128,1152]{2,1,0:T(8,128)(2,1)S(1)}, bf16[2,128,1152]{2,1,0:T(8,128)(2,1)}, u32[]{:S(2)}, u32[]{:S(2)}) collective-permute-start(bf16[2,128,1152]{2,1,0:T(8,128)(2,1)S(1)} %slice_bitcast_fusion), channel_id=1, source_target_pairs={{64,0},{128,64},{192,128},{256,192},{320,256},{384,320},{448,384},... | collective-permute-start | bytes 1769480 | tf_op jit(solution)/shard_map/ppermute | solution.py:14
  13.8 63.5 %all-to-all-start = ((bf16[3,1,64,2,1152]{4,3,1,0,2:T(2,128)(2,1)}), bf16[3,1,64,2,1152]{4,3,1,0,2:T(2,128)(2,1)S(1)}, u32[]{:S(2)}, u32[]{:S(2)}) async-start(bf16[3,1,64,2,1152]{4,3,1,0,2:T(2,128)(2,1)} %copy.235), calls=%async_computation | async-start | bytes 1769472 | tf_op jit(solution)/shard_map/all_to_all | solution.py:104
  25.2 1.0 copy-start.10
  25.4 23.9 %copy-start.11 = (bf16[2,1152]{1,0:T(2,128)(2,1)S(1)}, bf16[2,1152]{1,0:T(2,128)(2,1)}, u32[]{:S(2)}) copy-start(bf16[2,1152]{1,0:T(2,128)(2,1)} %param.10) | copy-start | bytes 13828
  25.4 24.0 %copy-start.3 = (bf16[1,1,128,1152]{3,2,1,0:T(8,128)(2,1)S(1)}, bf16[1,1,128,1152]{3,2,1,0:T(8,128)(2,1)}, u32[]{:S(2)}) copy-start(bf16[1,1,128,1152]{3,2,1,0:T(8,128)(2,1)} %param.8) | copy-start | bytes 884740
  48.0 3.0 %copy-start.13 = (s32[1,1,64]{2,1,0:T(1,128)S(1)}, s32[1,1,64]{2,1,0:T(1,128)}, u32[]{:S(2)}) copy-start(s32[1,1,64]{2,1,0:T(1,128)} %param.13) | copy-start | bytes 772
  49.3 3.2 %copy-start.12 = (s32[1,2]{1,0:T(1,128)S(1)}, s32[1,2]{1,0:T(1,128)}, u32[]{:S(2)}) copy-start(s32[1,2]{1,0:T(1,128)} %param.11) | copy-start | bytes 28
  64.2 1.2 %copy-start.1 = (bf16[384,288]{0,1:T(8,128)(2,1)S(1)}, bf16[384,288]{0,1:T(8,128)(2,1)}, u32[]{:S(2)}) copy-start(bf16[384,288]{0,1:T(8,128)(2,1)} %copy.228) | copy-start | bytes 663556
  64.2 1.2 %copy-start.5 = (bf16[128,288]{0,1:T(8,128)(2,1)S(1)}, bf16[128,288]{0,1:T(8,128)(2,1)}, u32[]{:S(2)}) copy-start(bf16[128,288]{0,1:T(8,128)(2,1)} %copy.229) | copy-start | bytes 221188
  67.7 5.9 %copy-start.7 = (bf16[128,288]{0,1:T(8,128)(2,1)S(1)}, bf16[128,288]{0,1:T(8,128)(2,1)}, u32[]{:S(2)}) copy-start(bf16[128,288]{0,1:T(8,128)(2,1)} %copy.225) | copy-start | bytes 221188
  73.5 0.9 copy-start.9
  74.5 0.9 copy-start.6
  82.5 1.0 copy-start.2
  84.1 15.2 %copy-start.4 = (bf16[128,288]{0,1:T(8,128)(2,1)S(1)}, bf16[128,288]{0,1:T(8,128)(2,1)}, u32[]{:S(2)}) copy-start(bf16[128,288]{0,1:T(8,128)(2,1)} %copy.217) | copy-start | bytes 221188
  86.2 25.5 %all-to-all-start.1 = ((bf16[64,1,2,1152]{3,2,1,0:T(2,128)(2,1)}), bf16[64,1,2,1152]{3,2,1,0:T(2,128)(2,1)S(1)}, u32[]{:S(2)}, u32[]{:S(2)}) async-start(bf16[64,1,2,1152]{3,2,1,0:T(2,128)(2,1)} %reshape.208), calls=%async_computation.1 | async-start | bytes 589824 | tf_op jit(solution)/shard_map/all_to_all | solution.py:106
  99.3 0.9 copy-start.8
where the time goes:
time: 114 us; the launch traced here: 113 us
  starting transfers between devices  35.2 us (31%)
  local copies, waits for them, and re-layouts  32.6 us (29%)
  blocking collectives  21.8 us (19%)
  waiting for transfers between devices  10.8 us (9%)
  matrix products  7.96 us (7%)
  between operations  2.37 us (2%)
  other arithmetic  1.94 us (2%)
    all_gather x1, blocking collectives, on_device(): boxes = lax.all_gather(box_kv, 'cam', axis=2, tiled=True)  21.8 us
    all_to_all x1, starting transfers between devices, time_attention(): lax.all_to_all(regrouped, 'frame', split_axis=0, concat_axis=1, tiled=True)  13.1 us
    all_to_all x1, starting transfers between devices, time_attention(): lax.all_to_all(blocked, 'frame', split_axis=2, concat_axis=1, tiled=True)  11.3 us
    all_to_all x1, waiting for transfers between devices, time_attention(): lax.all_to_all(regrouped, 'frame', split_axis=0, concat_axis=1, tiled=True)  10.8 us
    ppermute x2, starting transfers between devices, from_behind(): return lax.ppermute(block, axis, route)  10.7 us
    slice x5, local copies, waits for them, and re-layouts, attend_groups(): value_rows[:, start:stop]  5.79 us
    dot_general x5, matrix products, attend(): jnp.einsum('hrk,khd->rhd', packed, value_heads, preferred_element_type=jn...  4.11 us
    slice x5, local copies, waits for them, and re-layouts, attend_groups(): key_rows[:, start:stop]  3.43 us
  transfers between devices with their start and end apart: 4, of which 1 were waited for; matrix products, arithmetic and copies ran while one was open for 27% of the time, Pallas kernels for 0%

commit v1 on v0

v1 whole, which is shorter than its diff:
```python
import functools
import math

import jax
import jax.numpy as jnp
from jax import lax
from jax.experimental import pallas as pl
from jax.experimental.pallas import tpu as pltpu
from jax.sharding import PartitionSpec as P

MESH = pl.DeviceIdType.MESH
HEADS = 16
ROWS = 128
WIDTH = 1152
HEAD_DIM = WIDTH // HEADS
TILE = 128
SCALE = 1.0 / math.sqrt(HEAD_DIM)
FAR = -1e30
BF16 = jnp.bfloat16
F32 = jnp.float32
PARTS = ((0, 3), (3, 6), (6, 9))


def head_window(head):
    low = head * HEAD_DIM
    first = low // TILE
    last = (low + HEAD_DIM - 1) // TILE
    return low, first, last + 1


def heads_and_tiles():
    plan = []
    head_done = tile_done = 0
    for _, high in PARTS:
        heads = (high * TILE) // HEAD_DIM
        tiles = WIDTH // TILE if heads == HEADS else (heads * HEAD_DIM) // TILE
        plan.append((range(head_done, heads), (tile_done, tiles)))
        head_done, tile_done = heads, tiles
    return plan


def cols(first, last):
    return pl.ds(first * TILE, (last - first) * TILE)


def attend_heads(heads, q_ref, k_ref, v_ref, bias, emit, tiles):
    for head in heads:
        low, first, last = head_window(head)
        span = (last - first) * TILE
        lane = lax.broadcasted_iota(jnp.int32, (1, span), 1) + first * TILE
        mine = (lane >= low) & (lane < low + HEAD_DIM)
        window = pl.ds(first * TILE, span)
        q = q_ref[:, window] * mine.astype(F32).astype(BF16)
        scores = lax.dot_general(
            q, k_ref[:, window], (((1,), (1,)), ((), ())), preferred_element_type=F32
        )
        scores = scores + bias
        top = jnp.max(scores, axis=1, keepdims=True)
        weights = jnp.exp((scores - top) * SCALE)
        total = jnp.sum(weights, axis=1, keepdims=True)
        result = jnp.dot(weights.astype(BF16), v_ref[:, window], preferred_element_type=F32)
        result = result * (1.0 / total)
        for tile in range(first, last):
            at = (tile - first) * TILE
            part = result[:, at : at + TILE]
            if tile in tiles:
                part = jnp.where(mine[:, at : at + TILE], part, tiles[tile])
            tiles[tile] = part
            if low + HEAD_DIM >= (tile + 1) * TILE:
                emit(tile, tiles.pop(tile))


def kernel(
    qkv, cross_q, box_kv, null_kv, view_link, box_counts, box_visible, out,
    q_own, kv_all, z_in, z_perm, home, t_out, t_in, t_perm, t_fin,
    cq, boxes, nulls, ckv, vl, bc, bv, bv_wide, acc,
    local_sem, z_send, z_recv, xy_send, xy_recv, rxy_send, rxy_recv, rz_send, rz_recv,
    view_send, view_recv, box_send, box_recv, pair_send, pair_recv, own_sem,
):
    cam = lax.axis_index("cam")
    frame = lax.axis_index("frame")
    x, y, z = frame // 16, (frame // 8) % 2, frame % 8
    half = x % 2
    spot = half * 2 + y

    def z_peer(d):
        return (cam, x * 16 + y * 8 + (z + d) % 8)

    def spot_of(dx, dy):
        return ((half + dx) % 2) * 2 + (y + dy) % 2

    def xy_peer(dx, dy):
        return (cam, ((x // 2) * 2 + (half + dx) % 2) * 16 + ((y + dy) % 2) * 8 + z)

    def cam_peer(d):
        return ((cam + d) % 8, frame)

    pair = ((cam // 2) * 2 + (cam + 1) % 2, frame)
    z_order = (1, 7, 2, 6, 3, 5, 4)
    xy_order = ((0, 1), (1, 0), (1, 1))

    barrier = pltpu.get_barrier_semaphore()
    peers = [z_peer(d) for d in z_order] + [xy_peer(*d) for d in xy_order]
    peers += [cam_peer(d) for d in (1, 7, 2, 6, 4)]
    for peer in peers:
        pl.semaphore_signal(barrier, inc=1, device_id=peer, device_id_type=MESH)

    def rows16(i):
        return pl.ds(pl.multiple_of(i * 16, 16), 16)

    def rows32(i):
        return pl.ds(pl.multiple_of(i * 32, 32), 32)

    local = []
    for src, dst in (
        (box_kv, boxes.at[cam]),
        (null_kv, nulls),
        (view_link, vl),
        (box_counts, bc),
        (box_visible, bv),
        (cross_q, cq),
        (qkv.at[:, rows16(z)], z_in.at[:, rows16(z)]),
        (qkv.at[0], q_own),
        (qkv.at[pl.ds(1, 2)], kv_all.at[:, pl.ds(0, ROWS)]),
    ):
        copy = pltpu.make_async_copy(src, dst, local_sem.at[len(local)])
        copy.start()
        local.append(copy)

    pl.semaphore_wait(barrier, len(peers))

    def remote(src, dst, send, recv, peer):
        copy = pltpu.make_async_remote_copy(
            src_ref=src, dst_ref=dst, send_sem=send, recv_sem=recv, device_id=peer,
            device_id_type=MESH,
        )
        copy.start()
        return copy

    sent = []

    def send_z(part):
        first, last = PARTS[part]
        copies = []
        for i, d in enumerate(z_order):
            copies.append(
                remote(
                    qkv.at[:, rows16((z + d) % 8), cols(first, last)],
                    z_in.at[:, rows16(z), cols(first, last)],
                    z_send.at[part, i], z_recv.at[part, i], z_peer(d),
                )
            )
        sent.extend(copies)
        return copies

    z_copies = [send_z(0)]
    box_copies = []
    for i, d in enumerate((2, 6, 4)):
        box_copies.append(
            remote(box_kv, boxes.at[cam], box_send.at[i], box_recv.at[i], cam_peer(d))
        )
    pair_copies = [remote(box_kv, boxes.at[cam], pair_send.at[0], pair_recv.at[0], pair)]
    view_copies = []
    for i, d in enumerate((1, 7)):
        view_copies.append(
            remote(
                qkv.at[pl.ds(1, 2)], kv_all.at[:, pl.ds(ROWS * (i + 1), ROWS)],
                view_send.at[i], view_recv.at[i], cam_peer(d),
            )
        )
    z_copies.append(send_z(1))
    z_copies.append(send_z(2))

    for i, d in enumerate((2, 6, 4)):
        box_copies[i].wait_recv()
        block = boxes.at[(cam + 8 - d) % 8]
        pair_copies.append(
            remote(block, block, pair_send.at[i + 1], pair_recv.at[i + 1], pair)
        )

    row = lax.broadcasted_iota(jnp.int32, (ROWS, ROWS), 0)
    col = lax.broadcasted_iota(jnp.int32, (ROWS, ROWS), 1)

    def by_group(r):
        return ((r >> 2) & 7) * 16 + (r >> 5) * 4 + (r & 3)

    to_group = (col == by_group(row)).astype(F32).astype(BF16)
    to_frame = (row == by_group(col)).astype(F32).astype(BF16)
    same_patch = jnp.where(((row ^ col) & 3) == 0, 0.0, FAR).astype(F32)

    for copy in local:
        copy.wait()
    for copy in pair_copies:
        copy.wait_recv()

    ckv[...] = jnp.zeros_like(ckv)
    for t in range(2):
        slots = jnp.concatenate([boxes[c, t].astype(F32) for c in range(8)], axis=0)
        ckv[t, 0:64, :] = slots.astype(BF16)
        first_row = lax.broadcasted_iota(jnp.int32, (16, WIDTH), 0) == 0
        null_row = jnp.broadcast_to(nulls[t : t + 1, :].astype(F32), (16, WIDTH))
        ckv[t, 64:80, :] = jnp.where(first_row, null_row, 0.0).astype(BF16)
    bv_wide[...] = jnp.zeros_like(bv_wide)
    bv_wide[:, 0:64] = bv[...]
    lane = lax.broadcasted_iota(jnp.int32, (1, ROWS), 1)
    live = ((lane < bc[...]) & (bv_wide[...] == 1)) | (lane == 64)
    cross_bias = jnp.where(live, 0.0, FAR).astype(F32)

    def emit_cross(tile, value):
        acc[:, cols(tile, tile + 1)] = value

    attend_heads(range(HEADS), cq, ckv.at[0], ckv.at[1], cross_bias, emit_cross, {})

    plan = heads_and_tiles()

    def permute_in(part):
        for copy in z_copies[part]:
            copy.wait_recv()
        first, last = PARTS[part]
        for t in range(3):
            moved = jnp.dot(to_group, z_in[t, :, cols(first, last)], preferred_element_type=F32)
            z_perm[t, :, cols(first, last)] = moved.astype(BF16)
        copies = []
        for i, d in enumerate(xy_order):
            copies.append(
                remote(
                    z_perm.at[:, rows32(spot_of(*d)), cols(first, last)],
                    home.at[:, rows32(spot), cols(first, last)],
                    xy_send.at[part, i], xy_recv.at[part, i], xy_peer(*d),
                )
            )
        own = pltpu.make_async_copy(
            z_perm.at[:, rows32(spot), cols(first, last)],
            home.at[:, rows32(spot), cols(first, last)],
            own_sem.at[0, part],
        )
        own.start()
        sent.extend(copies)
        return copies, own

    half_tiles = {}

    def emit_time(tile, value):
        t_out[:, cols(tile, tile + 1)] = value.astype(BF16)

    def time_heads(part, arriving):
        copies, own = arriving
        for copy in copies:
            copy.wait_recv()
        own.wait()
        heads, (first, last) = plan[part]
        attend_heads(heads, home.at[0], home.at[1], home.at[2], same_patch, emit_time, half_tiles)
        back = []
        for i, d in enumerate(xy_order):
            back.append(
                remote(
                    t_out.at[rows32(spot_of(*d)), cols(first, last)],
                    t_in.at[rows32(spot), cols(first, last)],
                    rxy_send.at[part, i], rxy_recv.at[part, i], xy_peer(*d),
                )
            )
        mine = pltpu.make_async_copy(
            t_out.at[rows32(spot), cols(first, last)],
            t_in.at[rows32(spot), cols(first, last)],
            own_sem.at[1, part],
        )
        mine.start()
        sent.extend(back)
        return back, mine

    def permute_back(part, arriving):
        copies, own = arriving
        for copy in copies:
            copy.wait_recv()
        own.wait()
        _, (first, last) = plan[part]
        moved = jnp.dot(to_frame, t_in[:, cols(first, last)], preferred_element_type=F32)
        t_perm[:, cols(first, last)] = moved.astype(BF16)
        back = []
        for i, d in enumerate(z_order):
            back.append(
                remote(
                    t_perm.at[rows16((z + d) % 8), cols(first, last)],
                    t_fin.at[rows16(z), cols(first, last)],
                    rz_send.at[part, i], rz_recv.at[part, i], z_peer(d),
                )
            )
        mine = pltpu.make_async_copy(
            t_perm.at[rows16(z), cols(first, last)],
            t_fin.at[rows16(z), cols(first, last)],
            own_sem.at[2, part],
        )
        mine.start()
        sent.extend(back)
        return back, mine

    def finish(part, arriving):
        copies, own = arriving
        for copy in copies:
            copy.wait_recv()
        own.wait()
        _, (first, last) = plan[part]
        at = cols(first, last)
        out[:, at] = (acc[:, at] + t_fin[:, at].astype(F32)).astype(BF16)

    def emit_view(tile, value):
        at = cols(tile, tile + 1)
        acc[:, at] = acc[:, at] + value

    view_tiles = {}

    def view_heads(heads):
        linked = jnp.concatenate(
            [
                jnp.zeros((1, ROWS), F32),
                jnp.broadcast_to(jnp.where(vl[:, 0:1] == 1, 0.0, FAR).astype(F32), (1, ROWS)),
                jnp.broadcast_to(jnp.where(vl[:, 1:2] == 1, 0.0, FAR).astype(F32), (1, ROWS)),
            ],
            axis=1,
        )
        attend_heads(heads, q_own, kv_all.at[0], kv_all.at[1], linked, emit_view, view_tiles)

    xy0 = permute_in(0)
    xy1 = permute_in(1)
    r0 = time_heads(0, xy0)
    xy2 = permute_in(2)
    r1 = time_heads(1, xy1)
    f0 = permute_back(0, r0)
    for copy in view_copies:
        copy.wait_recv()
    view_heads(range(8))
    r2 = time_heads(2, xy2)
    f1 = permute_back(1, r1)
    view_heads(range(8, HEADS))
    f2 = permute_back(2, r2)
    finish(0, f0)
    finish(1, f1)
    finish(2, f2)
    for copy in sent + box_copies + pair_copies + view_copies:
        copy.wait_send()


def on_device(qkv, cross_q, box_kv, null_kv, view_link, box_counts, box_visible):
    parts = len(PARTS)
    dma = pltpu.SemaphoreType.DMA
    wide = (ROWS, WIDTH)
    blended = pl.pallas_call(
        kernel,
        out_shape=jax.ShapeDtypeStruct(wide, BF16),
        in_specs=[pl.BlockSpec(memory_space=pl.ANY)] * 7,
        out_specs=pl.BlockSpec(memory_space=pltpu.VMEM),
        scratch_shapes=[
            pltpu.VMEM(wide, BF16),
            pltpu.VMEM((2, 3 * ROWS, WIDTH), BF16),
            pltpu.VMEM((3,) + wide, BF16),
            pltpu.VMEM((3,) + wide, BF16),
            pltpu.VMEM((3,) + wide, BF16),
            pltpu.VMEM(wide, BF16),
            pltpu.VMEM(wide, BF16),
            pltpu.VMEM(wide, BF16),
            pltpu.VMEM(wide, BF16),
            pltpu.VMEM(wide, BF16),
            pltpu.VMEM((8, 2, 8, WIDTH), BF16),
            pltpu.VMEM((2, WIDTH), BF16),
            pltpu.VMEM((2,) + wide, BF16),
            pltpu.VMEM((1, 2), jnp.int32),
            pltpu.VMEM((1, 1), jnp.int32),
            pltpu.VMEM((1, 64), jnp.int32),
            pltpu.VMEM((1, 128), jnp.int32),
            pltpu.VMEM(wide, F32),
            dma((9,)),
            dma((parts, 7)),
            dma((parts, 7)),
            dma((parts, 3)),
            dma((parts, 3)),
            dma((parts, 3)),
            dma((parts, 3)),
            dma((parts, 7)),
            dma((parts, 7)),
            dma((2,)),
            dma((2,)),
            dma((3,)),
            dma((3,)),
            dma((4,)),
            dma((4,)),
            dma((3, parts)),
        ],
        compiler_params=pltpu.CompilerParams(
            collective_id=0, has_side_effects=True, vmem_limit_bytes=40 << 20
        ),
        name="multiview_attention",
    )(
        qkv[:, 0, 0],
        cross_q[0, 0],
        box_kv[:, 0],
        null_kv,
        view_link,
        box_counts.reshape(1, 1),
        box_visible[0],
    )
    return blended[None, None]


def solution(mesh):
    return jax.shard_map(
        on_device,
        mesh=mesh,
        in_specs=(
            P(None, "cam", "frame", None, None),
            P("cam", "frame", None, None),
            P(None, "frame", "cam", None),
            P(None, None),
            P("cam", None),
            P("frame"),
            P("cam", "frame", None),
        ),
        out_specs=P("cam", "frame", None, None),
        check_vma=False,
    )
```

time: 114 us -> 58.7 us (0.51)
  Pallas kernels: 0 us -> 53.1 us
  starting transfers between devices: 35.2 us -> 0 us
  local copies, waits for them, and re-layouts: 32.6 us -> 4.28 us
  blocking collectives: 21.8 us -> 0 us
  waiting for transfers between devices: 10.8 us -> 0 us
  matrix products: 7.96 us -> 0 us
  other arithmetic: 1.94 us -> 0 us
  between operations: 2.37 us -> 0.69 us
    pallas_call x0 -> x1, Pallas kernels: none -> 53.1 us  [on_device(): pl.pallas_call(kernel, out_shape=jax.ShapeDtypeStruct(wide, BF16), in_spe...]
    all_to_all x2 -> x0, starting transfers between devices: 24.4 us -> none  [the longest x1 13.1 us: time_attention(): lax.all_to_all(regrouped, 'frame', split_axis=0, concat_axis=1, tiled=True)]
    all_gather x1 -> x0, blocking collectives: 21.8 us -> none  [on_device(): boxes = lax.all_gather(box_kv, 'cam', axis=2, tiled=True)]
    slice x21 -> x0, local copies, waits for them, and re-layouts: 15.1 us -> none  [the longest x5 5.79 us: attend_groups(): value_rows[:, start:stop]]
    all_to_all x2 -> x0, waiting for transfers between devices: 10.8 us -> none  [the longest x1 10.8 us: time_attention(): lax.all_to_all(regrouped, 'frame', split_axis=0, concat_axis=1, tiled=True)]
    ppermute x2 -> x0, starting transfers between devices: 10.7 us -> none  [from_behind(): return lax.ppermute(block, axis, route)]
    dot_general x12 -> x0, matrix products: 7.96 us -> none  [the longest x5 4.11 us: attend(): jnp.einsum('hrk,khd->rhd', packed, value_heads, preferred_element_type=jn...]
    squeeze x6 -> x0, local copies, waits for them, and re-layouts: 6.29 us -> none  [the longest x2 2.2 us: view_attention(): key_rows = jnp.concatenate([key_value[0], left_pair[0], right_pair[0]], 0)]
  transfers between devices with their start and end apart: 4 -> 0, of which waited for: 1 -> 0; matrix products, arithmetic and copies ran while one was open for 27% -> 0% of each run, Pallas kernels for 0% -> 0%
where the time goes in v1:
time: 58.7 us; the launch traced here: 58 us
  Pallas kernels  53.1 us (90%)
  local copies, waits for them, and re-layouts  4.28 us (7%)
  between operations  0.69 us (1%)
    pallas_call x1, Pallas kernels, on_device(): pl.pallas_call(kernel, out_shape=jax.ShapeDtypeStruct(wide, BF16), in_spe...  53.1 us
    unnamed x13, local copies, waits for them, and re-layouts  4.28 us

profile of v1, /device:TPU:1, one launch (start us, length us, event | category | flops | bytes accessed | tf_op | source)
XLA Modules:
  0.0 58.0 jit_solution(13138163533698558794)
XLA Ops:
  0.7 0.0 copy-start.3
  0.7 0.0 copy-start.4
  0.7 0.0 copy-start.5
  0.7 0.7 %copy-done.3 = bf16[2,1152]{1,0:T(2,128)(2,1)S(1)} copy-done((bf16[2,1152]{1,0:T(2,128)(2,1)S(1)}, bf16[2,1152]{1,0:T(2,128)(2,1)}, u32[]{:S(2)}) %copy-start.3) | copy-done | bytes 4632
  1.3 0.0 copy-done.4
  1.3 0.0 copy-done.5
  1.3 0.0 copy-start
  1.3 1.2 %copy-done = bf16[3,1,1,128,1152]{4,3,2,1,0:T(8,128)(2,1)S(1)} copy-done((bf16[3,1,1,128,1152]{4,3,2,1,0:T(8,128)(2,1)S(1)}, bf16[3,1,1,128,1152]{4,3,2,1,0:T(8,128)(2,1)}, u32[]{:S(2)}) %copy-start) | copy-done | bytes 884760
  2.5 0.0 copy-start.1
  2.5 1.0 %copy-done.1 = bf16[1,1,128,1152]{3,2,1,0:T(8,128)(2,1)S(1)} copy-done((bf16[1,1,128,1152]{3,2,1,0:T(8,128)(2,1)S(1)}, bf16[1,1,128,1152]{3,2,1,0:T(8,128)(2,1)}, u32[]{:S(2)}) %copy-start.1) | copy-done | bytes 294936
  3.5 0.0 copy-start.2
  3.5 0.8 %copy-done.2 = bf16[2,1,8,1152]{3,2,1,0:T(8,128)(2,1)S(1)} copy-done((bf16[2,1,8,1152]{3,2,1,0:T(8,128)(2,1)S(1)}, bf16[2,1,8,1152]{3,2,1,0:T(8,128)(2,1)}, u32[]{:S(2)}) %copy-start.2) | copy-done | bytes 36888
  4.2 53.1 %multiview_attention.1 = bf16[128,1152]{1,0:T(8,128)(2,1)S(1)} custom-call(bf16[3,128,1152]{2,1,0:T(8,128)(2,1)S(1)} %bitcast.8, bf16[128,1152]{1,0:T(8,128)(2,1)S(1)} %bitcast.9, bf16[2,8,1152]{2,1,0:T(8,128)(2,1)S(1)} %bitcast.10, bf16[2,1152]{1,0:T(2,128)(2,1)S(1)} %copy-done.3, s32[1,2]{1,0:T(1,128)S(1)} %copy-done.4, s32[1,1]{1,0:T(1,128)} %bitcast.6.box_counts, ...), custom_call_target="tpu_custom_call" | custom-call | tf_op jit(solution)/shard_map/multiview_attention/pallas_call | solution.py:347
  57.3 0.7 %copy.10 = bf16[1,1,128,1152]{3,2,1,0:T(8,128)(2,1)} copy(bf16[1,1,128,1152]{3,2,1,0:T(8,128)(2,1)S(1)} %bitcast.7) | data formatting | bytes 589824
Async XLA Ops:
  0.7 0.7 %copy-start.3 = (bf16[2,1152]{1,0:T(2,128)(2,1)S(1)}, bf16[2,1152]{1,0:T(2,128)(2,1)}, u32[]{:S(2)}) copy-start(bf16[2,1152]{1,0:T(2,128)(2,1)} %null_kv.1) | copy-start | bytes 13828
  0.7 0.7 %copy-start.4 = (s32[1,2]{1,0:T(1,128)S(1)}, s32[1,2]{1,0:T(1,128)}, u32[]{:S(2)}) copy-start(s32[1,2]{1,0:T(1,128)} %view_link.1) | copy-start | bytes 28
  0.7 0.7 %copy-start.5 = (s32[1,1,64]{2,1,0:T(1,128)S(1)}, s32[1,1,64]{2,1,0:T(1,128)}, u32[]{:S(2)}) copy-start(s32[1,1,64]{2,1,0:T(1,128)} %param.13) | copy-start | bytes 772
  1.3 1.2 %copy-start = (bf16[3,1,1,128,1152]{4,3,2,1,0:T(8,128)(2,1)S(1)}, bf16[3,1,1,128,1152]{4,3,2,1,0:T(8,128)(2,1)}, u32[]{:S(2)}) copy-start(bf16[3,1,1,128,1152]{4,3,2,1,0:T(8,128)(2,1)} %param.7) | copy-start | bytes 2654212
  2.5 1.0 %copy-start.1 = (bf16[1,1,128,1152]{3,2,1,0:T(8,128)(2,1)S(1)}, bf16[1,1,128,1152]{3,2,1,0:T(8,128)(2,1)}, u32[]{:S(2)}) copy-start(bf16[1,1,128,1152]{3,2,1,0:T(8,128)(2,1)} %param.8) | copy-start | bytes 884740
  3.5 0.8 %copy-start.2 = (bf16[2,1,8,1152]{3,2,1,0:T(8,128)(2,1)S(1)}, bf16[2,1,8,1152]{3,2,1,0:T(8,128)(2,1)}, u32[]{:S(2)}) copy-start(bf16[2,1,8,1152]{3,2,1,0:T(8,128)(2,1)} %param.9) | copy-start | bytes 110596

commit v2 on v1

v2 whole, which is shorter than its diff:
```python
import functools
import math

import jax
import jax.numpy as jnp
from jax import lax
from jax.experimental import pallas as pl
from jax.experimental.pallas import tpu as pltpu
from jax.sharding import PartitionSpec as P

MESH = pl.DeviceIdType.MESH
HEADS = 16
ROWS = 128
WIDTH = 1152
HEAD_DIM = WIDTH // HEADS
TILE = 128
SCALE = 1.0 / math.sqrt(HEAD_DIM)
FAR = -1e30
BF16 = jnp.bfloat16
F32 = jnp.float32
PARTS = ((0, 3), (3, 7), (7, 9))


def head_window(head):
    low = head * HEAD_DIM
    first = low // TILE
    last = (low + HEAD_DIM - 1) // TILE
    return low, first, last + 1


def heads_and_tiles():
    plan = []
    head_done = tile_done = 0
    for _, high in PARTS:
        heads = (high * TILE) // HEAD_DIM
        tiles = WIDTH // TILE if heads == HEADS else (heads * HEAD_DIM) // TILE
        plan.append((range(head_done, heads), (tile_done, tiles)))
        head_done, tile_done = heads, tiles
    return plan


def cols(first, last):
    return pl.ds(first * TILE, (last - first) * TILE)


def attend_heads(heads, q_ref, k_ref, v_ref, bias, emit, tiles):
    for head in heads:
        low, first, last = head_window(head)
        span = (last - first) * TILE
        lane = lax.broadcasted_iota(jnp.int32, (1, span), 1) + first * TILE
        mine = (lane >= low) & (lane < low + HEAD_DIM)
        window = pl.ds(first * TILE, span)
        q = q_ref[:, window] * mine.astype(F32).astype(BF16)
        scores = lax.dot_general(
            q, k_ref[:, window], (((1,), (1,)), ((), ())), preferred_element_type=F32
        )
        scores = scores + bias
        top = jnp.max(scores, axis=1, keepdims=True)
        weights = jnp.exp((scores - top) * SCALE)
        total = jnp.sum(weights, axis=1, keepdims=True)
        result = jnp.dot(weights.astype(BF16), v_ref[:, window], preferred_element_type=F32)
        result = result * (1.0 / total)
        for tile in range(first, last):
            at = (tile - first) * TILE
            part = result[:, at : at + TILE]
            if tile in tiles:
                part = jnp.where(mine[:, at : at + TILE], part, tiles[tile])
            tiles[tile] = part
            if low + HEAD_DIM >= (tile + 1) * TILE:
                emit(tile, tiles.pop(tile))


def kernel(
    qkv, cross_q, box_kv, null_kv, view_link, box_counts, box_visible, out,
    q_own, kv_all, z_in, near_out, near_in, far_out, early, home, t_out, t_in, t_group, t_fin,
    cq, boxes, nulls, ckv, vl, bc, bv, bv_wide, acc,
    local_sem, z_send, z_recv, xy_send, xy_recv, rxy_send, rxy_recv, rz_send, rz_recv,
    view_send, view_recv, box_send, box_recv, pair_send, pair_recv, own_sem,
):
    cam = lax.axis_index("cam")
    frame = lax.axis_index("frame")
    x, y, z = frame // 16, (frame // 8) % 2, frame % 8
    half = x % 2
    spot = half * 2 + y

    def z_peer(d):
        return (cam, x * 16 + y * 8 + (z + d) % 8)

    def spot_of(dx, dy):
        return ((half + dx) % 2) * 2 + (y + dy) % 2

    def xy_peer(dx, dy):
        return (cam, ((x // 2) * 2 + (half + dx) % 2) * 16 + ((y + dy) % 2) * 8 + z)

    def cam_peer(d):
        return ((cam + d) % 8, frame)

    pair = ((cam // 2) * 2 + (cam + 1) % 2, frame)
    z_order = (4, 3, 5, 2, 6, 1, 7)
    xy_order = ((1, 1), (0, 1), (1, 0))

    barrier = pltpu.get_barrier_semaphore()
    peers = [z_peer(d) for d in z_order] + [cam_peer(d) for d in (4, 2, 6, 1, 7)]
    peers += [xy_peer(*d) for d in xy_order]
    for peer in peers:
        pl.semaphore_signal(barrier, inc=1, device_id=peer, device_id_type=MESH)

    def rows16(i):
        return pl.ds(pl.multiple_of(i * 16, 16), 16)

    def rows32(i):
        return pl.ds(pl.multiple_of(i * 32, 32), 32)

    def local_copy(src, dst, sem):
        copy = pltpu.make_async_copy(src, dst, sem)
        copy.start()
        return copy

    local = []
    for src, dst in (
        (qkv.at[0], q_own),
        (qkv.at[pl.ds(1, 2)], kv_all.at[:, pl.ds(0, ROWS)]),
        (qkv.at[:, rows16(z)], z_in.at[:, rows16(z)]),
        (cross_q, cq),
        (box_kv, boxes.at[cam]),
        (null_kv, nulls),
        (view_link, vl),
        (box_counts, bc),
        (box_visible, bv),
    ):
        local.append(local_copy(src, dst, local_sem.at[len(local)]))

    row = lax.broadcasted_iota(jnp.int32, (ROWS, ROWS), 0)
    col = lax.broadcasted_iota(jnp.int32, (ROWS, ROWS), 1)

    def by_group(r):
        return ((r >> 2) & 7) * 16 + (r >> 5) * 4 + (r & 3)

    to_group = (col == by_group(row)).astype(F32).astype(BF16)
    to_frame = (row == by_group(col)).astype(F32).astype(BF16)
    same_patch = jnp.where(((row ^ col) & 3) == 0, 0.0, FAR).astype(F32)

    def reorder(matrix, values):
        return jnp.dot(matrix, values, preferred_element_type=F32)

    pl.semaphore_wait(barrier, len(peers))

    sent = []

    def remote(src, dst, send, recv, peer):
        copy = pltpu.make_async_remote_copy(
            src_ref=src, dst_ref=dst, send_sem=send, recv_sem=recv, device_id=peer,
            device_id_type=MESH,
        )
        copy.start()
        sent.append(copy)
        return copy

    def arrive(copies):
        for copy in copies:
            if any(copy is one for one in sent):
                copy.wait_recv()
            else:
                copy.wait()

    plan = heads_and_tiles()

    def send_z(part, source):
        at = cols(*PARTS[part])
        target = z_in if part == 0 else home
        copies = [
            remote(
                source.at[:, rows16((z + d) % 8), at], target.at[:, rows16(z), at],
                z_send.at[part, i], z_recv.at[part, i], z_peer(d),
            )
            for i, d in enumerate(z_order)
        ]
        if part > 0:
            copies.append(
                local_copy(
                    source.at[:, rows16(z), at], target.at[:, rows16(z), at], own_sem.at[0, part]
                )
            )
        return copies

    def send_xy(part):
        at = cols(*PARTS[part])
        target = early if part == 0 else near_in
        copies = [
            remote(
                near_out.at[:, rows32(spot_of(*d)), at], target.at[:, rows32(spot), at],
                xy_send.at[part, i], xy_recv.at[part, i], xy_peer(*d),
            )
            for i, d in enumerate(xy_order)
        ]
        copies.append(
            local_copy(
                near_out.at[:, rows32(spot), at], target.at[:, rows32(spot), at],
                own_sem.at[1, part],
            )
        )
        return copies

    def group_own(part):
        at = cols(*PARTS[part])
        near_out[0, :, at] = reorder(to_group, q_own[:, at]).astype(BF16)
        for t in range(2):
            near_out[t + 1, :, at] = reorder(to_group, kv_all[t, 0:ROWS, at]).astype(BF16)
        return send_xy(part)

    def group_first(copies):
        arrive(copies)
        at = cols(*PARTS[0])
        for t in range(3):
            near_out[t, :, at] = reorder(to_group, z_in[t, :, at]).astype(BF16)
        return send_xy(0)

    def spread(part, copies):
        arrive(copies)
        at = cols(*PARTS[part])
        for t in range(3):
            far_out[t, :, at] = reorder(to_frame, near_in[t, :, at]).astype(BF16)
        return send_z(part, far_out)

    half_tiles = {}

    def emit_time(tile, value):
        t_out[:, cols(tile, tile + 1)] = value.astype(BF16)

    def time_heads(part, copies):
        arrive(copies)
        if part == 0:
            at = cols(*PARTS[0])
            for t in range(3):
                home[t, :, at] = reorder(to_frame, early[t, :, at]).astype(BF16)
        heads, tiles = plan[part]
        attend_heads(heads, home.at[0], home.at[1], home.at[2], same_patch, emit_time, half_tiles)
        at = cols(*tiles)
        back = [
            remote(
                t_out.at[rows16((z + d) % 8), at], t_in.at[rows16(z), at],
                rz_send.at[part, i], rz_recv.at[part, i], z_peer(d),
            )
            for i, d in enumerate(z_order)
        ]
        back.append(
            local_copy(t_out.at[rows16(z), at], t_in.at[rows16(z), at], own_sem.at[2, part])
        )
        return back

    def group_back(part, copies):
        arrive(copies)
        at = cols(*plan[part][1])
        t_group[:, at] = reorder(to_group, t_in[:, at]).astype(BF16)
        back = [
            remote(
                t_group.at[rows32(spot_of(*d)), at], t_fin.at[rows32(spot), at],
                rxy_send.at[part, i], rxy_recv.at[part, i], xy_peer(*d),
            )
            for i, d in enumerate(xy_order)
        ]
        back.append(
            local_copy(t_group.at[rows32(spot), at], t_fin.at[rows32(spot), at], own_sem.at[3, part])
        )
        return back

    def finish(part, copies):
        arrive(copies)
        at = cols(*plan[part][1])
        out[:, at] = (acc[:, at] + reorder(to_frame, t_fin[:, at])).astype(BF16)

    def cross_attention(copies):
        arrive(copies)
        ckv[...] = jnp.zeros_like(ckv)
        for t in range(2):
            slots = jnp.concatenate([boxes[c, t].astype(F32) for c in range(8)], axis=0)
            ckv[t, 0:64, :] = slots.astype(BF16)
            first_row = lax.broadcasted_iota(jnp.int32, (16, WIDTH), 0) == 0
            null_row = jnp.broadcast_to(nulls[t : t + 1, :].astype(F32), (16, WIDTH))
            ckv[t, 64:80, :] = jnp.where(first_row, null_row, 0.0).astype(BF16)
        bv_wide[...] = jnp.zeros_like(bv_wide)
        bv_wide[:, 0:64] = bv[...]
        lane = lax.broadcasted_iota(jnp.int32, (1, ROWS), 1)
        live = ((lane < bc[...]) & (bv_wide[...] == 1)) | (lane == 64)
        cross_bias = jnp.where(live, 0.0, FAR).astype(F32)

        def emit_cross(tile, value):
            acc[:, cols(tile, tile + 1)] = value

        attend_heads(range(HEADS), cq, ckv.at[0], ckv.at[1], cross_bias, emit_cross, {})

    def emit_view(tile, value):
        at = cols(tile, tile + 1)
        acc[:, at] = acc[:, at] + value

    view_tiles = {}

    def view_heads(heads):
        linked = jnp.concatenate(
            [
                jnp.zeros((1, ROWS), F32),
                jnp.broadcast_to(jnp.where(vl[:, 0:1] == 1, 0.0, FAR).astype(F32), (1, ROWS)),
                jnp.broadcast_to(jnp.where(vl[:, 1:2] == 1, 0.0, FAR).astype(F32), (1, ROWS)),
            ],
            axis=1,
        )
        attend_heads(heads, q_own, kv_all.at[0], kv_all.at[1], linked, emit_view, view_tiles)

    z0 = send_z(0, qkv)
    arrive(local[0:2])
    xy1 = group_own(1)
    xy2 = group_own(2)
    box_copies = [
        remote(box_kv, boxes.at[cam], box_send.at[i], box_recv.at[i], cam_peer(d))
        for i, d in enumerate((2, 6, 4))
    ]
    pair_copies = [remote(box_kv, boxes.at[cam], pair_send.at[0], pair_recv.at[0], pair)]
    view_copies = [
        remote(
            qkv.at[pl.ds(1, 2)], kv_all.at[:, pl.ds(ROWS * (i + 1), ROWS)],
            view_send.at[i], view_recv.at[i], cam_peer(d),
        )
        for i, d in enumerate((1, 7))
    ]
    z1 = spread(1, xy1)
    arrive(box_copies)
    for i, d in enumerate((2, 6, 4)):
        block = boxes.at[(cam + 8 - d) % 8]
        pair_copies.append(
            remote(block, block, pair_send.at[i + 1], pair_recv.at[i + 1], pair)
        )
    z2 = spread(2, xy2)
    cross_attention(local[3:] + pair_copies)
    xy0 = group_first(z0 + local[2:3])
    r0 = time_heads(0, xy0)
    arrive(view_copies)
    view_heads(range(5))
    r1 = time_heads(1, z1)
    f0 = group_back(0, r0)
    view_heads(range(5, 10))
    r2 = time_heads(2, z2)
    f1 = group_back(1, r1)
    view_heads(range(10, HEADS))
    f2 = group_back(2, r2)
    finish(0, f0)
    finish(1, f1)
    finish(2, f2)
    for copy in sent:
        copy.wait_send()


def on_device(qkv, cross_q, box_kv, null_kv, view_link, box_counts, box_visible):
    parts = len(PARTS)
    dma = pltpu.SemaphoreType.DMA
    wide = (ROWS, WIDTH)
    blended = pl.pallas_call(
        kernel,
        out_shape=jax.ShapeDtypeStruct(wide, BF16),
        in_specs=[pl.BlockSpec(memory_space=pltpu.HBM)] * 7,
        out_specs=pl.BlockSpec(memory_space=pltpu.VMEM),
        scratch_shapes=[
            pltpu.VMEM(wide, BF16),
            pltpu.VMEM((2, 3 * ROWS, WIDTH), BF16),
            pltpu.VMEM((3,) + wide, BF16),
            pltpu.VMEM((3,) + wide, BF16),
            pltpu.VMEM((3,) + wide, BF16),
            pltpu.VMEM((3,) + wide, BF16),
            pltpu.VMEM((3,) + wide, BF16),
            pltpu.VMEM((3,) + wide, BF16),
            pltpu.VMEM(wide, BF16),
            pltpu.VMEM(wide, BF16),
            pltpu.VMEM(wide, BF16),
            pltpu.VMEM(wide, BF16),
            pltpu.VMEM(wide, BF16),
            pltpu.VMEM((8, 2, 8, WIDTH), BF16),
            pltpu.VMEM((2, WIDTH), BF16),
            pltpu.VMEM((2,) + wide, BF16),
            pltpu.VMEM((1, 2), jnp.int32),
            pltpu.VMEM((1, 1), jnp.int32),
            pltpu.VMEM((1, 64), jnp.int32),
            pltpu.VMEM((1, 128), jnp.int32),
            pltpu.VMEM(wide, F32),
            dma((9,)),
            dma((parts, 7)),
            dma((parts, 7)),
            dma((parts, 3)),
            dma((parts, 3)),
            dma((parts, 3)),
            dma((parts, 3)),
            dma((parts, 7)),
            dma((parts, 7)),
            dma((2,)),
            dma((2,)),
            dma((3,)),
            dma((3,)),
            dma((4,)),
            dma((4,)),
            dma((4, parts)),
        ],
        compiler_params=pltpu.CompilerParams(
            collective_id=0, has_side_effects=True, vmem_limit_bytes=56 << 20
        ),
        name="multiview_attention",
    )(
        qkv[:, 0, 0],
        cross_q[0, 0],
        box_kv[:, 0],
        null_kv,
        view_link,
        box_counts.reshape(1, 1),
        box_visible[0],
    )
    return blended[None, None]


def solution(mesh):
    return jax.shard_map(
        on_device,
        mesh=mesh,
        in_specs=(
            P(None, "cam", "frame", None, None),
            P("cam", "frame", None, None),
            P(None, "frame", "cam", None),
            P(None, None),
            P("cam", None),
            P("frame"),
            P("cam", "frame", None),
        ),
        out_specs=P("cam", "frame", None, None),
        check_vma=False,
    )
```

time: 58.7 us -> 63.5 us (1.082)
  Pallas kernels: 53.1 us -> 59.9 us
  local copies, waits for them, and re-layouts: 4.28 us -> 1.7 us
    pallas_call x1, Pallas kernels: 53.1 us -> 59.9 us  [on_device(): pl.pallas_call(kernel, out_shape=jax.ShapeDtypeStruct(wide, BF16), in_spe...]
    unnamed x13 -> x1, local copies, waits for them, and re-layouts: 4.28 us -> 1.7 us
where the time goes in v2:
time: 63.5 us; the launch traced here: 62.2 us
  Pallas kernels  59.9 us (94%)
  local copies, waits for them, and re-layouts  1.7 us (3%)
  between operations  0.66 us (1%)
    pallas_call x1, Pallas kernels, on_device(): pl.pallas_call(kernel, out_shape=jax.ShapeDtypeStruct(wide, BF16), in_spe...  59.9 us
    unnamed x1, local copies, waits for them, and re-layouts  1.7 us

profile of v2, /device:TPU:1, one launch (start us, length us, event | category | flops | bytes accessed | tf_op | source)
XLA Modules:
  0.0 62.2 jit_solution(124837243157707355)
XLA Ops:
  0.7 59.9 %multiview_attention.1 = bf16[128,1152]{1,0:T(8,128)(2,1)} custom-call(bf16[3,128,1152]{2,1,0:T(8,128)(2,1)} %bitcast.8, bf16[128,1152]{1,0:T(8,128)(2,1)} %bitcast.9, bf16[2,8,1152]{2,1,0:T(8,128)(2,1)} %bitcast.10, bf16[2,1152]{1,0:T(2,128)(2,1)} %null_kv.1, s32[1,2]{1,0:T(1,128)} %view_link.1, s32[1,1]{1,0:T(1,128)} %bitcast.6.box_counts, s32[1,64]{1,0:T(1,128)} %bitcast.11), custom_call_target="tpu_custom_call" | custom-call | tf_op jit(solution)/shard_map/multiview_attention/pallas_call | solution.py:356
  60.5 1.7 %copy.10 = bf16[1,1,128,1152]{3,2,1,0:T(8,128)(2,1)} copy(bf16[1,1,128,1152]{3,2,1,0:T(8,128)(2,1)} %bitcast.7) | data formatting | bytes 589824

commit v3 on v2

--- a/solution.py
+++ b/solution.py
@@ -19,6 +19,7 @@
 BF16 = jnp.bfloat16
 F32 = jnp.float32
 PARTS = ((0, 3), (3, 7), (7, 9))
+VIEW_PIECES = ((0, 3), (3, 6), (6, 9))
 
 
 def head_window(head):
@@ -43,31 +44,47 @@
     return pl.ds(first * TILE, (last - first) * TILE)
 
 
+GROUP = 8
+
+
 def attend_heads(heads, q_ref, k_ref, v_ref, bias, emit, tiles):
-    for head in heads:
-        low, first, last = head_window(head)
-        span = (last - first) * TILE
-        lane = lax.broadcasted_iota(jnp.int32, (1, span), 1) + first * TILE
-        mine = (lane >= low) & (lane < low + HEAD_DIM)
-        window = pl.ds(first * TILE, span)
-        q = q_ref[:, window] * mine.astype(F32).astype(BF16)
-        scores = lax.dot_general(
-            q, k_ref[:, window], (((1,), (1,)), ((), ())), preferred_element_type=F32
-        )
-        scores = scores + bias
-        top = jnp.max(scores, axis=1, keepdims=True)
-        weights = jnp.exp((scores - top) * SCALE)
-        total = jnp.sum(weights, axis=1, keepdims=True)
-        result = jnp.dot(weights.astype(BF16), v_ref[:, window], preferred_element_type=F32)
-        result = result * (1.0 / total)
-        for tile in range(first, last):
-            at = (tile - first) * TILE
-            part = result[:, at : at + TILE]
-            if tile in tiles:
-                part = jnp.where(mine[:, at : at + TILE], part, tiles[tile])
-            tiles[tile] = part
-            if low + HEAD_DIM >= (tile + 1) * TILE:
-                emit(tile, tiles.pop(tile))
+    heads = list(heads)
+    for start in range(0, len(heads), GROUP):
+        group = heads[start : start + GROUP]
+        windows, owned, scores = [], [], []
+        for head in group:
+            low, first, last = head_window(head)
+            span = (last - first) * TILE
+            lane = lax.broadcasted_iota(jnp.int32, (1, span), 1) + first * TILE
+            mine = (lane >= low) & (lane < low + HEAD_DIM)
+            window = pl.ds(first * TILE, span)
+            q = q_ref[:, window] * mine.astype(F32).astype(BF16)
+            windows.append(window)
+            owned.append(mine)
+            scores.append(
+                lax.dot_general(
+                    q, k_ref[:, window], (((1,), (1,)), ((), ())), preferred_element_type=F32
+                )
+            )
+        scores = [score + bias for score in scores]
+        tops = [jnp.max(score, axis=1, keepdims=True) for score in scores]
+        weights = [jnp.exp((score - top) * SCALE) for score, top in zip(scores, tops)]
+        totals = [jnp.sum(weight, axis=1, keepdims=True) for weight in weights]
+        results = [
+            jnp.dot(weight.astype(BF16), v_ref[:, window], preferred_element_type=F32)
+            for weight, window in zip(weights, windows)
+        ]
+        results = [result * (1.0 / total) for result, total in zip(results, totals)]
+        for head, mine, result in zip(group, owned, results):
+            low, first, last = head_window(head)
+            for tile in range(first, last):
+                at = (tile - first) * TILE
+                part = result[:, at : at + TILE]
+                if tile in tiles:
+                    part = jnp.where(mine[:, at : at + TILE], part, tiles[tile])
+                tiles[tile] = part
+                if low + HEAD_DIM >= (tile + 1) * TILE:
+                    emit(tile, tiles.pop(tile))
 
 
 def kernel(
@@ -306,6 +323,19 @@
         )
         attend_heads(heads, q_own, kv_all.at[0], kv_all.at[1], linked, emit_view, view_tiles)
 
+    odd = cam % 2
+    far_peer = ((cam + 7 - 6 * odd) % 8, frame)
+
+    def view_rows(slot):
+        return pl.ds(pl.multiple_of(slot * ROWS, ROWS), ROWS)
+
+    def send_far_view(piece):
+        at = cols(*VIEW_PIECES[piece])
+        return remote(
+            qkv.at[pl.ds(1, 2), :, at], kv_all.at[:, view_rows(2 - odd), at],
+            view_send.at[piece + 1], view_recv.at[piece + 1], far_peer,
+        )
+
     z0 = send_z(0, qkv)
     arrive(local[0:2])
     xy1 = group_own(1)
@@ -317,29 +347,32 @@
     pair_copies = [remote(box_kv, boxes.at[cam], pair_send.at[0], pair_recv.at[0], pair)]
     view_copies = [
         remote(
-            qkv.at[pl.ds(1, 2)], kv_all.at[:, pl.ds(ROWS * (i + 1), ROWS)],
-            view_send.at[i], view_recv.at[i], cam_peer(d),
-        )
-        for i, d in enumerate((1, 7))
+            qkv.at[pl.ds(1, 2)], kv_all.at[:, view_rows(1 + odd)], view_send.at[0],
+            view_recv.at[0], pair,
+        )
     ]
     z1 = spread(1, xy1)
+    z2 = spread(2, xy2)
     arrive(box_copies)
     for i, d in enumerate((2, 6, 4)):
         block = boxes.at[(cam + 8 - d) % 8]
         pair_copies.append(
             remote(block, block, pair_send.at[i + 1], pair_recv.at[i + 1], pair)
         )
-    z2 = spread(2, xy2)
+    xy0 = group_first(z0 + local[2:3])
+    for piece in range(len(VIEW_PIECES)):
+        view_copies.append(send_far_view(piece))
     cross_attention(local[3:] + pair_copies)
-    xy0 = group_first(z0 + local[2:3])
     r0 = time_heads(0, xy0)
-    arrive(view_copies)
-    view_heads(range(5))
     r1 = time_heads(1, z1)
+    arrive(view_copies[0:2])
+    view_heads(range(0, 5))
+    r2 = time_heads(2, z2)
+    arrive(view_copies[2:3])
+    view_heads(range(5, 10))
     f0 = group_back(0, r0)
-    view_heads(range(5, 10))
-    r2 = time_heads(2, z2)
     f1 = group_back(1, r1)
+    arrive(view_copies[3:4])
     view_heads(range(10, HEADS))
     f2 = group_back(2, r2)
     finish(0, f0)
@@ -389,8 +422,8 @@
             dma((parts, 3)),
             dma((parts, 7)),
             dma((parts, 7)),
-            dma((2,)),
-            dma((2,)),
+            dma((1 + len(VIEW_PIECES),)),
+            dma((1 + len(VIEW_PIECES),)),
             dma((3,)),
             dma((3,)),
             dma((4,)),

time: 63.5 us -> 54.3 us (0.86); the launches traced: 62.2 us -> 53.7 us
  Pallas kernels: 59.9 us -> 51.3 us
    pallas_call x1, Pallas kernels: 59.9 us -> 51.3 us  [on_device(): pl.pallas_call(kernel, out_shape=jax.ShapeDtypeStruct(wide, BF16), in_spe...]
where the time goes in v3:
time: 54.3 us; the launch traced here: 53.7 us
  Pallas kernels  51.3 us (94%)
  local copies, waits for them, and re-layouts  1.7 us (3%)
  between operations  0.66 us (1%)
    pallas_call x1, Pallas kernels, on_device(): pl.pallas_call(kernel, out_shape=jax.ShapeDtypeStruct(wide, BF16), in_spe...  51.3 us
    unnamed x1, local copies, waits for them, and re-layouts  1.7 us

profile of v3, /device:TPU:1, one launch (start us, length us, event | category | flops | bytes accessed | tf_op | source)
XLA Modules:
  0.0 53.7 jit_solution(16170757186352415443)
XLA Ops:
  0.7 51.3 %multiview_attention.1 = bf16[128,1152]{1,0:T(8,128)(2,1)} custom-call(bf16[3,128,1152]{2,1,0:T(8,128)(2,1)} %bitcast.8, bf16[128,1152]{1,0:T(8,128)(2,1)} %bitcast.9, bf16[2,8,1152]{2,1,0:T(8,128)(2,1)} %bitcast.10, bf16[2,1152]{1,0:T(2,128)(2,1)} %null_kv.1, s32[1,2]{1,0:T(1,128)} %view_link.1, s32[1,1]{1,0:T(1,128)} %bitcast.6.box_counts, s32[1,64]{1,0:T(1,128)} %bitcast.11), custom_call_target="tpu_custom_call" | custom-call | tf_op jit(solution)/shard_map/multiview_attention/pallas_call | solution.py:389
  52.0 1.7 %copy.10 = bf16[1,1,128,1152]{3,2,1,0:T(8,128)(2,1)} copy(bf16[1,1,128,1152]{3,2,1,0:T(8,128)(2,1)} %bitcast.7) | data formatting | bytes 589824

commit v4 on v3

--- a/solution.py
+++ b/solution.py
@@ -133,19 +133,10 @@
         copy.start()
         return copy
 
-    local = []
-    for src, dst in (
-        (qkv.at[0], q_own),
-        (qkv.at[pl.ds(1, 2)], kv_all.at[:, pl.ds(0, ROWS)]),
-        (qkv.at[:, rows16(z)], z_in.at[:, rows16(z)]),
-        (cross_q, cq),
-        (box_kv, boxes.at[cam]),
-        (null_kv, nulls),
-        (view_link, vl),
-        (box_counts, bc),
-        (box_visible, bv),
-    ):
-        local.append(local_copy(src, dst, local_sem.at[len(local)]))
+    local = [
+        local_copy(qkv.at[0], q_own, local_sem.at[0]),
+        local_copy(qkv.at[pl.ds(1, 2)], kv_all.at[:, pl.ds(0, ROWS)], local_sem.at[1]),
+    ]
 
     row = lax.broadcasted_iota(jnp.int32, (ROWS, ROWS), 0)
     col = lax.broadcasted_iota(jnp.int32, (ROWS, ROWS), 1)
@@ -163,6 +154,13 @@
     pl.semaphore_wait(barrier, len(peers))
 
     sent = []
+    drained = []
+
+    def drain(copies):
+        for copy in copies:
+            if any(copy is one for one in sent) and not any(copy is one for one in drained):
+                copy.wait_send()
+                drained.append(copy)
 
     def remote(src, dst, send, recv, peer):
         copy = pltpu.make_async_remote_copy(
@@ -337,14 +335,24 @@
         )
 
     z0 = send_z(0, qkv)
-    arrive(local[0:2])
-    xy1 = group_own(1)
-    xy2 = group_own(2)
+    for src, dst in (
+        (qkv.at[:, rows16(z)], z_in.at[:, rows16(z)]),
+        (cross_q, cq),
+        (box_kv, boxes.at[cam]),
+        (null_kv, nulls),
+        (view_link, vl),
+        (box_counts, bc),
+        (box_visible, bv),
+    ):
+        local.append(local_copy(src, dst, local_sem.at[len(local)]))
     box_copies = [
         remote(box_kv, boxes.at[cam], box_send.at[i], box_recv.at[i], cam_peer(d))
         for i, d in enumerate((2, 6, 4))
     ]
     pair_copies = [remote(box_kv, boxes.at[cam], pair_send.at[0], pair_recv.at[0], pair)]
+    arrive(local[0:2])
+    xy1 = group_own(1)
+    xy2 = group_own(2)
     view_copies = [
         remote(
             qkv.at[pl.ds(1, 2)], kv_all.at[:, view_rows(1 + odd)], view_send.at[0],
@@ -367,19 +375,27 @@
     r1 = time_heads(1, z1)
     arrive(view_copies[0:2])
     view_heads(range(0, 5))
+    drain(z0 + xy1 + xy2 + box_copies + pair_copies)
     r2 = time_heads(2, z2)
     arrive(view_copies[2:3])
     view_heads(range(5, 10))
+    drain(z1 + xy0 + view_copies[0:2])
     f0 = group_back(0, r0)
+    drain(z2 + r0 + view_copies)
     f1 = group_back(1, r1)
     arrive(view_copies[3:4])
     view_heads(range(10, HEADS))
+    drain(r1 + f0)
     f2 = group_back(2, r2)
     finish(0, f0)
     finish(1, f1)
+    drain(r2 + f1)
     finish(2, f2)
-    for copy in sent:
-        copy.wait_send()
+    drain(sent)
+
+
+def in_hbm(operand):
+    return pltpu.with_memory_space_constraint(operand, pltpu.HBM)
 
 
 def on_device(qkv, cross_q, box_kv, null_kv, view_link, box_counts, box_visible):
@@ -389,7 +405,7 @@
     blended = pl.pallas_call(
         kernel,
         out_shape=jax.ShapeDtypeStruct(wide, BF16),
-        in_specs=[pl.BlockSpec(memory_space=pltpu.HBM)] * 7,
+        in_specs=[pl.BlockSpec(memory_space=pl.ANY)] * 7,
         out_specs=pl.BlockSpec(memory_space=pltpu.VMEM),
         scratch_shapes=[
             pltpu.VMEM(wide, BF16),
@@ -431,17 +447,17 @@
             dma((4, parts)),
         ],
         compiler_params=pltpu.CompilerParams(
-            collective_id=0, has_side_effects=True, vmem_limit_bytes=56 << 20
+            collective_id=0, has_side_effects=True, vmem_limit_bytes=40 << 20
         ),
         name="multiview_attention",
     )(
-        qkv[:, 0, 0],
-        cross_q[0, 0],
-        box_kv[:, 0],
-        null_kv,
-        view_link,
+        in_hbm(qkv[:, 0, 0]),
+        in_hbm(cross_q[0, 0]),
+        in_hbm(box_kv[:, 0]),
+        in_hbm(null_kv),
+        in_hbm(view_link),
         box_counts.reshape(1, 1),
-        box_visible[0],
+        in_hbm(box_visible[0]),
     )
     return blended[None, None]
 

time: 54.3 us -> 52.4 us (0.965)
  local copies, waits for them, and re-layouts: 1.7 us -> 0.72 us
  Pallas kernels: 51.3 us -> 50.7 us
    unnamed x1, local copies, waits for them, and re-layouts: 1.7 us -> 0.72 us
    pallas_call x1, Pallas kernels: 51.3 us -> 50.7 us  [on_device(): pl.pallas_call(kernel, out_shape=jax.ShapeDtypeStruct(wide, BF16), in_spe...]
where the time goes in v4:
time: 52.4 us; the launch traced here: 52.1 us
  Pallas kernels  50.7 us (97%)
  local copies, waits for them, and re-layouts  0.72 us (1%)
  between operations  0.66 us (1%)
    pallas_call x1, Pallas kernels, on_device(): pl.pallas_call(kernel, out_shape=jax.ShapeDtypeStruct(wide, BF16), in_spe...  50.7 us

profile of v4, /device:TPU:1, one launch (start us, length us, event | category | flops | bytes accessed | tf_op | source)
XLA Modules:
  0.0 52.1 jit_solution(1683716698132246445)
XLA Ops:
  0.7 50.7 %multiview_attention.1 = bf16[128,1152]{1,0:T(8,128)(2,1)S(1)} custom-call(bf16[3,128,1152]{2,1,0:T(8,128)(2,1)} %bitcast.8, bf16[128,1152]{1,0:T(8,128)(2,1)} %bitcast.9, bf16[2,8,1152]{2,1,0:T(8,128)(2,1)} %bitcast.10, bf16[2,1152]{1,0:T(2,128)(2,1)} %null_kv.1, s32[1,2]{1,0:T(1,128)} %view_link.1, s32[1,1]{1,0:T(1,128)} %bitcast.6.box_counts, ...), custom_call_target="tpu_custom_call" | custom-call | tf_op jit(solution)/shard_map/multiview_attention/pallas_call | solution.py:405
  51.4 0.7 %copy.10 = bf16[1,1,128,1152]{3,2,1,0:T(8,128)(2,1)} copy(bf16[1,1,128,1152]{3,2,1,0:T(8,128)(2,1)S(1)} %bitcast.7) | data formatting | bytes 589824

commit v5 on v4

--- a/solution.py
+++ b/solution.py
@@ -19,7 +19,7 @@
 BF16 = jnp.bfloat16
 F32 = jnp.float32
 PARTS = ((0, 3), (3, 7), (7, 9))
-VIEW_PIECES = ((0, 3), (3, 6), (6, 9))
+VIEW_PIECES = ((0, 3), (3, 7), (7, 9))
 
 
 def head_window(head):
@@ -345,14 +345,14 @@
         (box_visible, bv),
     ):
         local.append(local_copy(src, dst, local_sem.at[len(local)]))
+    arrive(local[0:2])
+    xy1 = group_own(1)
+    xy2 = group_own(2)
     box_copies = [
         remote(box_kv, boxes.at[cam], box_send.at[i], box_recv.at[i], cam_peer(d))
         for i, d in enumerate((2, 6, 4))
     ]
     pair_copies = [remote(box_kv, boxes.at[cam], pair_send.at[0], pair_recv.at[0], pair)]
-    arrive(local[0:2])
-    xy1 = group_own(1)
-    xy2 = group_own(2)
     view_copies = [
         remote(
             qkv.at[pl.ds(1, 2)], kv_all.at[:, view_rows(1 + odd)], view_send.at[0],
@@ -361,30 +361,30 @@
     ]
     z1 = spread(1, xy1)
     z2 = spread(2, xy2)
+    xy0 = group_first(z0 + local[2:3])
+    for piece in range(len(VIEW_PIECES)):
+        view_copies.append(send_far_view(piece))
     arrive(box_copies)
     for i, d in enumerate((2, 6, 4)):
         block = boxes.at[(cam + 8 - d) % 8]
         pair_copies.append(
             remote(block, block, pair_send.at[i + 1], pair_recv.at[i + 1], pair)
         )
-    xy0 = group_first(z0 + local[2:3])
-    for piece in range(len(VIEW_PIECES)):
-        view_copies.append(send_far_view(piece))
-    cross_attention(local[3:] + pair_copies)
     r0 = time_heads(0, xy0)
     r1 = time_heads(1, z1)
+    cross_attention(local[3:] + pair_copies)
+    r2 = time_heads(2, z2)
+    drain(z0 + xy1 + xy2 + box_copies + pair_copies)
     arrive(view_copies[0:2])
     view_heads(range(0, 5))
-    drain(z0 + xy1 + xy2 + box_copies + pair_copies)
-    r2 = time_heads(2, z2)
+    f0 = group_back(0, r0)
+    drain(z1 + xy0 + view_copies[0:2])
     arrive(view_copies[2:3])
-    view_heads(range(5, 10))
-    drain(z1 + xy0 + view_copies[0:2])
-    f0 = group_back(0, r0)
+    view_heads(range(5, 12))
+    f1 = group_back(1, r1)
     drain(z2 + r0 + view_copies)
-    f1 = group_back(1, r1)
     arrive(view_copies[3:4])
-    view_heads(range(10, HEADS))
+    view_heads(range(12, HEADS))
     drain(r1 + f0)
     f2 = group_back(2, r2)
     finish(0, f0)

time: 52.4 us -> 50.2 us (0.958); the launches traced: 52.1 us -> 49.3 us
  Pallas kernels: 50.7 us -> 47.9 us
    pallas_call x1, Pallas kernels: 50.7 us -> 47.9 us  [on_device(): pl.pallas_call(kernel, out_shape=jax.ShapeDtypeStruct(wide, BF16), in_spe...]
where the time goes in v5:
time: 50.2 us; the launch traced here: 49.3 us
  Pallas kernels  47.9 us (95%)
  local copies, waits for them, and re-layouts  0.72 us (1%)
  between operations  0.66 us (1%)
    pallas_call x1, Pallas kernels, on_device(): pl.pallas_call(kernel, out_shape=jax.ShapeDtypeStruct(wide, BF16), in_spe...  47.9 us

profile of v5, /device:TPU:1, one launch (start us, length us, event | category | flops | bytes accessed | tf_op | source)
XLA Modules:
  0.0 49.3 jit_solution(9281626149342120590)
XLA Ops:
  0.7 47.9 %multiview_attention.1 = bf16[128,1152]{1,0:T(8,128)(2,1)S(1)} custom-call(bf16[3,128,1152]{2,1,0:T(8,128)(2,1)} %bitcast.8, bf16[128,1152]{1,0:T(8,128)(2,1)} %bitcast.9, bf16[2,8,1152]{2,1,0:T(8,128)(2,1)} %bitcast.10, bf16[2,1152]{1,0:T(2,128)(2,1)} %null_kv.1, s32[1,2]{1,0:T(1,128)} %view_link.1, s32[1,1]{1,0:T(1,128)} %bitcast.6.box_counts, ...), custom_call_target="tpu_custom_call" | custom-call | tf_op jit(solution)/shard_map/multiview_attention/pallas_call | solution.py:405
  48.6 0.7 %copy.10 = bf16[1,1,128,1152]{3,2,1,0:T(8,128)(2,1)} copy(bf16[1,1,128,1152]{3,2,1,0:T(8,128)(2,1)S(1)} %bitcast.7) | data formatting | bytes 589824

commit v6 on v5

--- a/solution.py
+++ b/solution.py
@@ -117,7 +117,7 @@
     xy_order = ((1, 1), (0, 1), (1, 0))
 
     barrier = pltpu.get_barrier_semaphore()
-    peers = [z_peer(d) for d in z_order] + [cam_peer(d) for d in (4, 2, 6, 1, 7)]
+    peers = [z_peer(d) for d in z_order] + [cam_peer(d) for d in (2, 6, 1, 7)]
     peers += [xy_peer(*d) for d in xy_order]
     for peer in peers:
         pl.semaphore_signal(barrier, inc=1, device_id=peer, device_id_type=MESH)
@@ -350,7 +350,7 @@
     xy2 = group_own(2)
     box_copies = [
         remote(box_kv, boxes.at[cam], box_send.at[i], box_recv.at[i], cam_peer(d))
-        for i, d in enumerate((2, 6, 4))
+        for i, d in enumerate((2, 6))
     ]
     pair_copies = [remote(box_kv, boxes.at[cam], pair_send.at[0], pair_recv.at[0], pair)]
     view_copies = [
@@ -362,18 +362,27 @@
     z1 = spread(1, xy1)
     z2 = spread(2, xy2)
     xy0 = group_first(z0 + local[2:3])
+    arrive(box_copies)
+    for i, (d, t) in enumerate(((2, 0), (6, 1))):
+        block = boxes.at[(cam + 8 - d) % 8, t]
+        box_copies.append(
+            remote(block, block, box_send.at[i + 2], box_recv.at[i + 2], cam_peer(d))
+        )
+
     for piece in range(len(VIEW_PIECES)):
         view_copies.append(send_far_view(piece))
-    arrive(box_copies)
-    for i, d in enumerate((2, 6, 4)):
+    def cross_chip(i, d):
         block = boxes.at[(cam + 8 - d) % 8]
-        pair_copies.append(
-            remote(block, block, pair_send.at[i + 1], pair_recv.at[i + 1], pair)
-        )
+        pair_copies.append(remote(block, block, pair_send.at[i], pair_recv.at[i], pair))
+
+    cross_chip(1, 2)
+    cross_chip(2, 6)
     r0 = time_heads(0, xy0)
     r1 = time_heads(1, z1)
+    arrive(box_copies[2:4])
+    cross_chip(3, 4)
+    r2 = time_heads(2, z2)
     cross_attention(local[3:] + pair_copies)
-    r2 = time_heads(2, z2)
     drain(z0 + xy1 + xy2 + box_copies + pair_copies)
     arrive(view_copies[0:2])
     view_heads(range(0, 5))
@@ -440,8 +449,8 @@
             dma((parts, 7)),
             dma((1 + len(VIEW_PIECES),)),
             dma((1 + len(VIEW_PIECES),)),
-            dma((3,)),
-            dma((3,)),
+            dma((4,)),
+            dma((4,)),
             dma((4,)),
             dma((4,)),
             dma((4, parts)),

time: 50.2 us -> 49.7 us (0.990); the launches traced: 49.3 us -> 49.5 us
  no operation moved by 1% of the time
where the time goes in v6:
time: 49.7 us; the launch traced here: 49.5 us
  Pallas kernels  48.2 us (97%)
  local copies, waits for them, and re-layouts  0.72 us (1%)
  between operations  0.66 us (1%)
    pallas_call x1, Pallas kernels, on_device(): pl.pallas_call(kernel, out_shape=jax.ShapeDtypeStruct(wide, BF16), in_spe...  48.2 us

profile of v6, /device:TPU:1, one launch (start us, length us, event | category | flops | bytes accessed | tf_op | source)
XLA Modules:
  0.0 49.5 jit_solution(11434798887096632509)
XLA Ops:
  0.7 48.2 %multiview_attention.1 = bf16[128,1152]{1,0:T(8,128)(2,1)S(1)} custom-call(bf16[3,128,1152]{2,1,0:T(8,128)(2,1)} %bitcast.8, bf16[128,1152]{1,0:T(8,128)(2,1)} %bitcast.9, bf16[2,8,1152]{2,1,0:T(8,128)(2,1)} %bitcast.10, bf16[2,1152]{1,0:T(2,128)(2,1)} %null_kv.1, s32[1,2]{1,0:T(1,128)} %view_link.1, s32[1,1]{1,0:T(1,128)} %bitcast.6.box_counts, ...), custom_call_target="tpu_custom_call" | custom-call | tf_op jit(solution)/shard_map/multiview_attention/pallas_call | solution.py:414
  48.8 0.7 %copy.10 = bf16[1,1,128,1152]{3,2,1,0:T(8,128)(2,1)} copy(bf16[1,1,128,1152]{3,2,1,0:T(8,128)(2,1)S(1)} %bitcast.7) | data formatting | bytes 589824

commit v7 on v6

--- a/solution.py
+++ b/solution.py
@@ -392,10 +392,10 @@
     view_heads(range(5, 12))
     f1 = group_back(1, r1)
     drain(z2 + r0 + view_copies)
+    drain(r1 + f0)
+    f2 = group_back(2, r2)
     arrive(view_copies[3:4])
     view_heads(range(12, HEADS))
-    drain(r1 + f0)
-    f2 = group_back(2, r2)
     finish(0, f0)
     finish(1, f1)
     drain(r2 + f1)

time: 49.7 us -> 49.2 us (0.990)
  Pallas kernels: 48.2 us -> 47.7 us
where the time goes in v7:
time: 49.2 us; the launch traced here: 49.1 us
  Pallas kernels  47.7 us (97%)
  local copies, waits for them, and re-layouts  0.72 us (1%)
  between operations  0.66 us (1%)
    pallas_call x1, Pallas kernels, on_device(): pl.pallas_call(kernel, out_shape=jax.ShapeDtypeStruct(wide, BF16), in_spe...  47.7 us

profile of v7, /device:TPU:1, one launch (start us, length us, event | category | flops | bytes accessed | tf_op | source)
XLA Modules:
  0.0 49.1 jit_solution(15203527086333574390)
XLA Ops:
  0.7 47.7 %multiview_attention.1 = bf16[128,1152]{1,0:T(8,128)(2,1)S(1)} custom-call(bf16[3,128,1152]{2,1,0:T(8,128)(2,1)} %bitcast.8, bf16[128,1152]{1,0:T(8,128)(2,1)} %bitcast.9, bf16[2,8,1152]{2,1,0:T(8,128)(2,1)} %bitcast.10, bf16[2,1152]{1,0:T(2,128)(2,1)} %null_kv.1, s32[1,2]{1,0:T(1,128)} %view_link.1, s32[1,1]{1,0:T(1,128)} %bitcast.6.box_counts, ...), custom_call_target="tpu_custom_call" | custom-call | tf_op jit(solution)/shard_map/multiview_attention/pallas_call | solution.py:414
  48.4 0.7 %copy.10 = bf16[1,1,128,1152]{3,2,1,0:T(8,128)(2,1)} copy(bf16[1,1,128,1152]{3,2,1,0:T(8,128)(2,1)S(1)} %bitcast.7) | data formatting | bytes 589824
